TPU v7x, 256 devices: a whole 4x4x8 slice. The times are simulated.
256 devices in a mesh: rep: 16 (over x_hi, y, core), work: 16 (over x_lo, z).
Axes of the slice: x: 4 (x_hi: 2, x_lo: 2; x = x_hi * 2 + x_lo), y: 4, z: 8, core: 2. Of those that a mesh axis runs over, the one named last changes fastest.
Arguments:
- grads: bfloat16 [8192, 10240], P(('rep', 'work')), may hold values from -6 to 6
- panels: bfloat16 [64, 512, 512], P('work'), may hold values from -0.25 to 0.25
- eigvals: bfloat16 [64, 512], P('work'), may hold values from 0.19921875 to 3
- owner_slot: int32 [56], replicated, may hold values from 0 to 63, as said below
Outputs:
- precond: bfloat16 [8192, 10240], P(('rep', 'work'))
Inputs may be any that keep to these rules, and one draw needn't show every extreme that they name: owner_slot holds distinct slot numbers; slot s lies on index s // 4 of work.
All inputs are finite; a program needn't handle non-finite values.
Results may differ from a plain program's by a relative error of at most 0.0054.
Values may be sent and summed in bfloat16 or wider, within the bound.
A program may use at most 64 MiB of HBM per device.

v0:
```python
import jax
import jax.numpy as jnp
from jax import lax
from jax.sharding import PartitionSpec as P

D = 4096
FF = 10240


damping = 0.2


def broadcast(block, axis, holder):
    block = jnp.where(lax.axis_index(axis) == holder, block, jnp.zeros_like(block))
    return lax.psum(block, axis)


def fetch(panels, eigvals, owner_slot, factor_index):
    slot_count = panels.shape[0]
    selected_slot = owner_slot[factor_index]
    panel_data = lax.dynamic_index_in_dim(panels, selected_slot % slot_count, 0, keepdims=False)
    value_data = lax.dynamic_index_in_dim(eigvals, selected_slot % slot_count, 0, keepdims=False)
    return (
        broadcast(panel_data, "work", selected_slot // slot_count),
        broadcast(value_data, "work", selected_slot // slot_count),
    )


def per_device(grads, panels, eigvals, owner_slot):
    workers = lax.axis_size("work")
    groups = lax.axis_size("rep")
    group_index = lax.axis_index("rep")
    member = lax.axis_index("work")
    row_count = grads.shape[0]
    block_size = row_count * workers
    right_count = FF // block_size
    layer_index = group_index * block_size // D
    first_right = groups + layer_index * right_count
    left_panel, left_values = fetch(panels, eigvals, owner_slot, group_index)
    columns = lax.all_to_all(grads, "work", split_axis=1, concat_axis=0, tiled=True)
    rotated = lax.dot_general(
        left_panel, columns, (((0,), (0,)), ((), ())), preferred_element_type=jnp.float32
    ).astype(jnp.bfloat16)
    row_form = lax.all_to_all(rotated, "work", split_axis=0, concat_axis=1, tiled=True)
    slot_count = panels.shape[0]
    slot_total = slot_count * workers
    right_slots = lax.dynamic_slice_in_dim(owner_slot, first_right, right_count)
    picker = (jnp.arange(slot_total, dtype=jnp.int32)[:, None] == right_slots[None, :]).astype(
        jnp.bfloat16
    )
    sections = row_form.reshape(row_count, right_count, block_size)
    outgoing = jnp.einsum(
        "sj,rjc->src", picker, sections, preferred_element_type=jnp.float32
    ).astype(jnp.bfloat16)
    outgoing = outgoing.reshape(workers, slot_count, row_count, block_size)
    incoming = lax.all_to_all(outgoing, "work", split_axis=0, concat_axis=0, tiled=True)
    full_values = left_values.astype(jnp.float32)
    finished_slots = []
    for local_slot in range(slot_count):
        whole = incoming[:, local_slot].reshape(block_size, block_size)
        in_use = jnp.any(right_slots == member * slot_count + local_slot)
        own_panel = panels[local_slot]
        own_values = eigvals[local_slot].astype(jnp.float32)

        def compute(entire, own_panel=own_panel, own_values=own_values):
            turned = jnp.dot(entire, own_panel, preferred_element_type=jnp.float32)
            scaled = (turned / (full_values[:, None] * own_values[None, :] + damping)).astype(
                jnp.bfloat16
            )
            return lax.dot_general(
                scaled, own_panel, (((1,), (1,)), ((), ())), preferred_element_type=jnp.float32
            ).astype(jnp.bfloat16)

        def nothing(entire):
            return jnp.zeros_like(entire)

        done = lax.cond(in_use, compute, nothing, whole)
        finished_slots.append(done.reshape(workers, row_count, block_size))
    returning = jnp.stack(finished_slots, axis=1)
    back = lax.all_to_all(returning, "work", split_axis=0, concat_axis=0, tiled=True).reshape(
        slot_total, row_count, block_size
    )
    chosen_rows = jnp.einsum(
        "sj,src->rjc", picker, back, preferred_element_type=jnp.float32
    ).astype(jnp.bfloat16)
    result = chosen_rows.reshape(row_count, right_count * block_size)
    gathered = lax.all_to_all(result, "work", split_axis=1, concat_axis=0, tiled=True)
    finished = jnp.dot(left_panel, gathered, preferred_element_type=jnp.float32).astype(
        jnp.bfloat16
    )
    return lax.all_to_all(finished, "work", split_axis=0, concat_axis=1, tiled=True)


def solution(mesh):
    return jax.shard_map(
        per_device,
        mesh=mesh,
        in_specs=(P(("rep", "work"), None), P("work", None, None), P("work", None), P()),
        out_specs=P(("rep", "work"), None),
        check_vma=False,
    )
```

profile of v0, /device:TPU:36, one launch (start us, length us, event | category | flops | bytes accessed | tf_op | source)
XLA Modules:
  0.0 349.5 jit_solution(5896310641531279353)
XLA Ops:
  6.5 2.0 copy.41
  8.5 9.2 %all-to-all-start = ((bf16[32,16,640]{2,0,1:T(8,128)(2,1)}), bf16[32,16,640]{2,0,1:T(8,128)(2,1)S(1)}, u32[]{:S(2)}, u32[]{:S(2)}) async-start(bf16[32,16,640]{2,0,1:T(8,128)(2,1)} %bitcast.67), calls=%async_computation | async-start | bytes 1310720 | tf_op jit(solution)/shard_map/all_to_all | solution.py:40
  20.7 1.9 select_bitcast_fusion
  22.6 135.6 %all-reduce.2.cloned.1.call-done = bf16[512,512]{1,0:T(8,128)(2,1)} async-done(((bf16[512,512]{1,0:T(8,128)(2,1)}), bf16[512,512]{1,0:T(8,128)(2,1)}) %all-reduce.2.cloned.1.call-update) | async-done | bytes 524304 | tf_op jit(solution)/shard_map/psum | solution.py:15
  158.2 2.5 convolution_convert_fusion.6
  160.7 5.4 %all-to-all-start.1 = ((bf16[16,32,640]{2,1,0:T(8,128)(2,1)}), bf16[16,32,640]{2,1,0:T(8,128)(2,1)S(1)}, u32[]{:S(2)}, u32[]{:S(2)}) async-start(bf16[16,32,640]{2,1,0:T(8,128)(2,1)} %bitcast.21), calls=%async_computation.1 | async-start | bytes 1310720 | tf_op jit(solution)/shard_map/all_to_all | solution.py:44
  166.9 10.9 %all-to-all-done.1 = bf16[16,32,640]{2,1,0:T(8,128)(2,1)S(1)} async-done(((bf16[16,32,640]{2,1,0:T(8,128)(2,1)}), bf16[16,32,640]{2,1,0:T(8,128)(2,1)S(1)}, u32[]{:S(2)}, u32[]{:S(2)}) %all-to-all-start.1) | async-done | bytes 655392 | tf_op jit(solution)/shard_map/all_to_all | solution.py:44
  179.4 2.5 copy.30
  182.0 5.9 %all-to-all-start.2 = ((bf16[16,4,32,512]{3,2,1,0:T(8,128)(2,1)}), bf16[16,4,32,512]{3,2,1,0:T(8,128)(2,1)S(1)}, u32[]{:S(2)}, u32[]{:S(2)}) async-start(bf16[16,4,32,512]{3,2,1,0:T(8,128)(2,1)} %bitcast.68), calls=%async_computation.2 | async-start | bytes 4194304 | tf_op jit(solution)/shard_map/all_to_all | solution.py:56
  190.5 58.3 %psum.15 = bf16[512]{0:T(512)(128)(2,1)S(1)} all-reduce(bf16[512]{0:T(512)(128)(2,1)S(1)} %fusion.57), channel_id=1, replica_groups=mesh['rep'=16,'work'=16] {'work'}, use_global_device_ids=true, to_apply=%region_2.3 | all-reduce | flops 512 | bytes 2048 | tf_op jit(solution)/shard_map/psum | solution.py:15
  248.9 2.9 conditional.6
  248.9 0.8 slice.42
  249.8 2.1 convolution_convert_fusion.2
  251.9 0.9 conditional.5
  251.9 0.8 stack_reshape.22
  252.7 2.9 conditional.4
  252.7 0.8 slice.36
  253.5 2.1 convolution_convert_fusion
  255.6 1.3 pad_maximum_fusion
  256.9 42.3 %all_to_all.83 = bf16[16,4,32,512]{3,2,1,0:T(8,128)(2,1)S(1)} all-to-all(bf16[16,4,32,512]{3,2,1,0:T(8,128)(2,1)S(1)} %pad_maximum_fusion), channel_id=1, replica_groups=mesh['rep'=16,'work'=16] {'work'}, dimensions={0} | all-to-all | bytes 4194304 | tf_op jit(solution)/shard_map/all_to_all | solution.py:80
  299.2 1.3 fusion.49
  301.2 19.6 %all_to_all.84 = bf16[32,16,640]{2,0,1:T(8,128)(2,1)S(1)} all-to-all(bf16[32,16,640]{2,0,1:T(8,128)(2,1)S(1)} %copy.28), channel_id=1, replica_groups=mesh['rep'=16,'work'=16] {'work'}, dimensions={1} | all-to-all | bytes 1310720 | tf_op jit(solution)/shard_map/all_to_all | solution.py:87
  321.4 20.4 %all_to_all.85 = bf16[16,32,640]{2,1,0:T(8,128)(2,1)S(1)} all-to-all(bf16[16,32,640]{2,1,0:T(8,128)(2,1)S(1)} %bitcast.83), channel_id=1, replica_groups=mesh['rep'=16,'work'=16] {'work'}, dimensions={0} | all-to-all | bytes 1310720 | tf_op jit(solution)/shard_map/all_to_all | solution.py:91
  341.8 0.9 copy.33
  (24 shorter events, 4.5 us)
Async XLA Ops:
  6.5 11.3 %copy-start.1 = (s32[56]{0:T(128)S(1)}, s32[56]{0:T(128)}, u32[]{:S(2)}) copy-start(s32[56]{0:T(128)} %param.15) | copy-start | bytes 676
  8.5 149.7 %all-to-all-start = ((bf16[32,16,640]{2,0,1:T(8,128)(2,1)}), bf16[32,16,640]{2,0,1:T(8,128)(2,1)S(1)}, u32[]{:S(2)}, u32[]{:S(2)}) async-start(bf16[32,16,640]{2,0,1:T(8,128)(2,1)} %bitcast.67), calls=%async_computation | async-start | bytes 1310720 | tf_op jit(solution)/shard_map/all_to_all | solution.py:40
  17.8 140.5 %all-reduce.2.cloned.1.call-start = ((), (), s32[]{:S(2)}) async-start(), calls=%async_computation.6 | async-start | bytes 1048576 | tf_op jit(solution)/shard_map/psum | solution.py:15
  160.7 17.1 %all-to-all-start.1 = ((bf16[16,32,640]{2,1,0:T(8,128)(2,1)}), bf16[16,32,640]{2,1,0:T(8,128)(2,1)S(1)}, u32[]{:S(2)}, u32[]{:S(2)}) async-start(bf16[16,32,640]{2,1,0:T(8,128)(2,1)} %bitcast.21), calls=%async_computation.1 | async-start | bytes 1310720 | tf_op jit(solution)/shard_map/all_to_all | solution.py:44
  182.0 8.5 %copy-start = (bf16[4,512]{1,0:T(4,128)(2,1)S(1)}, bf16[4,512]{1,0:T(4,128)(2,1)}, u32[]{:S(2)}) copy-start(bf16[4,512]{1,0:T(4,128)(2,1)} %param.14) | copy-start | bytes 12292
  182.0 66.9 %all-to-all-start.2 = ((bf16[16,4,32,512]{3,2,1,0:T(8,128)(2,1)}), bf16[16,4,32,512]{3,2,1,0:T(8,128)(2,1)S(1)}, u32[]{:S(2)}, u32[]{:S(2)}) async-start(bf16[16,4,32,512]{3,2,1,0:T(8,128)(2,1)} %bitcast.68), calls=%async_computation.2 | async-start | bytes 4194304 | tf_op jit(solution)/shard_map/all_to_all | solution.py:56
  300.5 20.3 %copy-start.2 = (bf16[512,512]{1,0:T(8,128)(2,1)S(1)}, bf16[512,512]{1,0:T(8,128)(2,1)}, u32[]{:S(2)}) copy-start(bf16[512,512]{1,0:T(8,128)(2,1)} %all-reduce.2.cloned.1.call-done) | copy-start | bytes 1572868
Sparse Core Ops, SparseCore 0:
  22.7 135.4 all-reduce.1
where the time goes:
time: 353 us; the launch traced here: 350 us
  waiting for transfers between devices  147 us (42%)
  blocking collectives  141 us (40%)
  starting transfers between devices  20.6 us (6%)
  between operations  18.4 us (5%)
  local copies, waits for them, and re-layouts  10.1 us (3%)
  matrix products  9.28 us (3%)
  other arithmetic  4.03 us (1%)
    psum x1, waiting for transfers between devices, broadcast(): return lax.psum(block, axis)  136 us
    psum x1, blocking collectives, broadcast(): return lax.psum(block, axis)  58.3 us
    all_to_all x1, blocking collectives, per_device(): lax.all_to_all(returning, 'work', split_axis=0, concat_axis=0, tiled=True)  42.3 us
    all_to_all x1, blocking collectives, per_device(): lax.all_to_all(finished, 'work', split_axis=0, concat_axis=1, tiled=True)  20.4 us
    all_to_all x1, blocking collectives, per_device(): lax.all_to_all(result, 'work', split_axis=1, concat_axis=0, tiled=True)  19.6 us
    all_to_all x1, waiting for transfers between devices, per_device(): lax.all_to_all(rotated, 'work', split_axis=0, concat_axis=1, tiled=True)  10.9 us
    all_to_all x1, starting transfers between devices, per_device(): lax.all_to_all(grads, 'work', split_axis=1, concat_axis=0, tiled=True)  9.22 us
  transfers between devices with their start and end apart: 4, of which 2 were waited for; matrix products, arithmetic and copies ran while one was open for 1% of the time, Pallas kernels for 0%

commit v1 on v0

v1 whole, which is shorter than its diff:
```python
import jax
import jax.numpy as jnp
from jax import lax
from jax.experimental import pallas as pl
from jax.experimental.pallas import tpu as pltpu
from jax.sharding import PartitionSpec as P

MESH = pl.DeviceIdType.MESH
N = 512
W = 16
Q = 8
ROWS = 32
RIGHT = 20
LEFT = 16
SLOTS = 4
EXTRA = RIGHT - W
DAMPING = 0.2
BF16 = jnp.bfloat16
F32 = jnp.float32


def partner(w, dx, dz):
    return ((w // 8 + dx) % 2) * 8 + (w % 8 + dz) % 8


def near_first(k):
    return jnp.where(k % 2 == 0, k // 2 + 1, 7 - k // 2)


def extra_home(e):
    return (e // 2) * 8 + (e % 2) * 4 + (e // 2) * 2


def tile(ref, i):
    return ref.at[i // 4, :, pl.ds(pl.multiple_of((i % 4) * 128, 128), 128)]


def kernel(
    owner, grads, panels, eigs, out,
    tiles, eig_all, eig_row, eig_mine, stage_s, stage_p, p_buf, s_buf, rx, tx, xs, us,
    sem_send, sem_t, sem_e, sem_p2, sem_p3, sem_s2, sem_s3, sem_g, sem_o,
):
    r = lax.axis_index("rep")
    w = lax.axis_index("work")
    layer = r // Q
    q = r % Q
    extra = jnp.int32(-1)
    for e in range(EXTRA):
        extra = jnp.where(w == extra_home(e), e, extra)
    has_extra = extra >= 0
    mine = jnp.where(has_extra, extra, 0)

    barrier = pltpu.get_barrier_semaphore()

    def others(body):
        @pl.loop(0, 7)
        def _(k):
            body(partner(w, 0, near_first(k)))

        body(partner(w, 1, 0))

        @pl.loop(0, 7)
        def _(k):
            body(partner(w, 1, near_first(k)))

    def mates(body):
        @pl.loop(1, Q)
        def _(k):
            body((q + k) % Q)

    def greet(t):
        pl.semaphore_signal(barrier, inc=1, device_id={"work": t}, device_id_type=MESH)

    def greet_mate(m):
        pl.semaphore_signal(barrier, inc=1, device_id={"rep": layer * Q + m}, device_id_type=MESH)

    others(greet)
    mates(greet_mate)

    def remote(src, dst, send, recv, **where):
        pltpu.make_async_remote_copy(
            src_ref=src, dst_ref=dst, send_sem=send, recv_sem=recv, device_id=where, device_id_type=MESH
        ).start()

    def local(src, dst, sem):
        pltpu.make_async_copy(src, dst, sem).start()

    def settle(ref, sem):
        pltpu.make_async_copy(ref, ref, sem).wait()

    values = eigs[...].astype(F32)
    for s in range(SLOTS):
        for c in range(4):
            eig_row[4 * s + c : 4 * s + c + 1, :] = values[s : s + 1, c * 128 : (c + 1) * 128]
    eig_mine[...] = eig_row[...].astype(BF16)

    pl.semaphore_wait(barrier, W - 1 + Q - 1)

    def piece_of(i):
        rows = pl.multiple_of(q * 64 + (i // 4) * 16, 16)
        return panels.at[:, pl.ds(rows, 16), pl.ds(pl.multiple_of((i % 4) * 128, 128), 128)]

    def send_tiles(t):
        remote(piece_of(t), tiles.at[pl.ds(w * SLOTS, SLOTS)], sem_send.at[0], sem_t, work=t)
        remote(eig_mine, eig_all.at[w], sem_send.at[1], sem_e, work=t)

    others(send_tiles)
    local(piece_of(w), tiles.at[pl.ds(w * SLOTS, SLOTS)], sem_t)
    local(eig_mine, eig_all.at[w], sem_e)

    def block_of(j):
        return grads.at[:, pl.ds(pl.multiple_of(j * N, N), N)]

    def row_slice(ref, u, k):
        return ref.at[u, pl.ds(pl.multiple_of(k * ROWS, ROWS), ROWS), :]

    def send_rows(t):
        remote(block_of(t), row_slice(rx, 0, w), sem_send.at[2], sem_g.at[0], work=t)

    others(send_rows)
    local(block_of(w), row_slice(rx, 0, w), sem_g.at[0])

    @pl.loop(0, EXTRA)
    def _(k):
        e = (k + w) % EXTRA
        home = extra_home(e)

        @pl.when(home != w)
        def _():
            remote(block_of(W + e), row_slice(rx, 1, w), sem_send.at[3], sem_g.at[1], work=home)

        @pl.when(home == w)
        def _():
            local(block_of(W + e), row_slice(rx, 1, w), sem_g.at[1])

    settle(tiles, sem_t)

    @pl.loop(0, Q)
    def _(m):
        stage_p[m] = tiles[owner[layer * Q + m]]

    def p_tile(k):
        return tile(p_buf.at[k], w)

    def send_p(m):
        remote(stage_p.at[m], p_tile(q), sem_send.at[4], sem_p2, rep=layer * Q + m)

    mates(send_p)
    local(stage_p.at[q], p_tile(q), sem_p2)

    @pl.loop(0, RIGHT)
    def _(j):
        stage_s[j] = tiles[owner[LEFT + layer * RIGHT + j]]

    def send_s(t):
        remote(stage_s.at[t], tile(s_buf.at[0, q], w), sem_send.at[5], sem_s2.at[0], work=t)

    others(send_s)
    local(stage_s.at[w], tile(s_buf.at[0, q], w), sem_s2.at[0])

    @pl.loop(0, EXTRA)
    def _(k):
        e = (k + w) % EXTRA
        home = extra_home(e)

        @pl.when(home != w)
        def _():
            remote(stage_s.at[W + e], tile(s_buf.at[1, q], w), sem_send.at[6], sem_s2.at[1], work=home)

        @pl.when(home == w)
        def _():
            local(stage_s.at[W + e], tile(s_buf.at[1, q], w), sem_s2.at[1])

    def p_share(k):
        return p_buf.at[:, k // 4, :, pl.ds(pl.multiple_of((k % 4) * 128, 128), 128)]

    settle(p_share(w), sem_p2)

    def send_share(t):
        remote(p_share(w), p_share(w), sem_send.at[7], sem_p3, work=t)

    others(send_share)

    settle(s_buf.at[0, q], sem_s2.at[0])

    def send_slab(m):
        remote(s_buf.at[0, q], s_buf.at[0, q], sem_send.at[8], sem_s3.at[0], rep=layer * Q + m)

    mates(send_slab)

    @pl.when(has_extra)
    def _():
        settle(s_buf.at[1, q], sem_s2.at[1])

        def send_slab_extra(m):
            remote(s_buf.at[1, q], s_buf.at[1, q], sem_send.at[9], sem_s3.at[1], rep=layer * Q + m)

        mates(send_slab_extra)

    settle(eig_all, sem_e)

    def values_of(slot):
        whole = eig_all[slot // SLOTS].astype(F32)
        part = slot % SLOTS
        picked = whole[0:4]
        for s in range(1, SLOTS):
            picked = jnp.where(part == s, whole[4 * s : 4 * s + 4], picked)
        return picked

    left = values_of(owner[r])
    columns = []
    for c in range(4):
        columns.append(jnp.transpose(jnp.broadcast_to(left[c : c + 1], (128, 128))))
    left_columns = jnp.concatenate(columns, axis=0)

    others_rows = rx.at[0, pl.ds(0, (W - 1) * ROWS), :]
    settle(others_rows, sem_p3)

    def out_block(j):
        return out.at[:, pl.ds(pl.multiple_of(j * N, N), N)]

    def compute(u, right):
        settle(s_buf.at[u, 0:7], sem_s3.at[u])
        settle(rx.at[u], sem_g.at[u])
        p = p_buf[...].reshape(N, N)
        s = s_buf[u].reshape(N, N)
        for c in range(2):
            cols = slice(c * 256, (c + 1) * 256)
            xs[:, cols] = lax.dot_general(
                p, rx[u, :, cols], (((0,), (0,)), ((), ())), preferred_element_type=F32
            ).astype(BF16)
        for c in range(4):
            cols = slice(c * 128, (c + 1) * 128)
            turned = jnp.dot(xs[...], s[:, cols], preferred_element_type=F32)
            us[:, cols] = (turned / (left_columns * right[c : c + 1] + DAMPING)).astype(BF16)
        for c in range(2):
            cols = slice(c * 256, (c + 1) * 256)
            back = lax.dot_general(
                us[...], s[cols], (((1,), (1,)), ((), ())), preferred_element_type=F32
            ).astype(BF16)
            tx[u, :, cols] = jnp.dot(p, back, preferred_element_type=F32).astype(BF16)

    right0 = values_of(owner[LEFT + layer * RIGHT + w])
    compute(0, right0)

    def send_out(t):
        remote(row_slice(tx, 0, t), out_block(w), sem_send.at[10], sem_o, work=t)

    others(send_out)
    local(row_slice(tx, 0, w), out_block(w), sem_o)

    @pl.when(has_extra)
    def _():
        right1 = values_of(owner[LEFT + layer * RIGHT + W + mine])
        compute(1, right1)

        def send_out_extra(t):
            remote(row_slice(tx, 1, t), out_block(W + mine), sem_send.at[11], sem_o, work=t)

        others(send_out_extra)
        local(row_slice(tx, 1, w), out_block(W + mine), sem_o)

    settle(tiles.at[0 : (W - 1) * SLOTS], sem_send.at[0])
    settle(eig_all.at[0 : W - 1], sem_send.at[1])
    settle(others_rows, sem_send.at[2])
    settle(stage_p.at[0 : Q - 1], sem_send.at[4])
    settle(stage_s.at[0 : W - 1], sem_send.at[5])
    settle(others_rows, sem_send.at[7])
    settle(s_buf.at[0, 0:7], sem_send.at[8])
    settle(others_rows, sem_send.at[10])

    @pl.when(has_extra)
    def _():
        settle(rx.at[0, pl.ds(0, (EXTRA - 1) * ROWS), :], sem_send.at[3])
        settle(stage_s.at[0 : EXTRA - 1], sem_send.at[6])
        settle(s_buf.at[1, 0:7], sem_send.at[9])
        settle(others_rows, sem_send.at[11])

    @pl.when(jnp.logical_not(has_extra))
    def _():
        settle(rx.at[0, pl.ds(0, EXTRA * ROWS), :], sem_send.at[3])
        settle(stage_s.at[0:EXTRA], sem_send.at[6])

    settle(out, sem_o)


def per_device(grads, panels, eigvals, owner_slot):
    return pl.pallas_call(
        kernel,
        out_shape=jax.ShapeDtypeStruct(grads.shape, BF16),
        in_specs=[
            pl.BlockSpec(memory_space=pltpu.SMEM),
            pl.BlockSpec(memory_space=pl.ANY),
            pl.BlockSpec(memory_space=pl.ANY),
            pl.BlockSpec(memory_space=pltpu.VMEM),
        ],
        out_specs=pl.BlockSpec(memory_space=pl.ANY),
        scratch_shapes=[
            pltpu.VMEM((W * SLOTS, 16, 128), BF16),
            pltpu.VMEM((W, 16, 128), BF16),
            pltpu.VMEM((16, 128), F32),
            pltpu.VMEM((16, 128), BF16),
            pltpu.VMEM((RIGHT, 16, 128), BF16),
            pltpu.VMEM((Q, 16, 128), BF16),
            pltpu.VMEM((Q, 4, 16, N), BF16),
            pltpu.VMEM((2, Q, 4, 16, N), BF16),
            pltpu.VMEM((2, N, N), BF16),
            pltpu.VMEM((2, N, N), BF16),
            pltpu.VMEM((N, N), BF16),
            pltpu.VMEM((N, N), BF16),
            pltpu.SemaphoreType.DMA((12,)),
            pltpu.SemaphoreType.DMA,
            pltpu.SemaphoreType.DMA,
            pltpu.SemaphoreType.DMA,
            pltpu.SemaphoreType.DMA,
            pltpu.SemaphoreType.DMA((2,)),
            pltpu.SemaphoreType.DMA((2,)),
            pltpu.SemaphoreType.DMA((2,)),
            pltpu.SemaphoreType.DMA,
        ],
        compiler_params=pltpu.CompilerParams(
            collective_id=0, has_side_effects=True, vmem_limit_bytes=32 * 1024 * 1024
        ),
    )(owner_slot, grads, panels, eigvals)


def solution(mesh):
    return jax.shard_map(
        per_device,
        mesh=mesh,
        in_specs=(P(("rep", "work"), None), P("work", None, None), P("work", None), P()),
        out_specs=P(("rep", "work"), None),
        check_vma=False,
    )
```

time: 353 us -> 75.1 us (0.21)
  the two profiles are of different devices: /device:TPU:36 before, /device:TPU:6 now
where the time goes in v1:
time: 75.1 us; the launch traced here: 74.9 us
  Pallas kernels  70 us (93%)
  local copies, waits for them, and re-layouts  4.86 us (6%)
    pallas_call x1, Pallas kernels, per_device(): pl.pallas_call(kernel, out_shape=jax.ShapeDtypeStruct(grads.shape, BF16),...  70 us
    unnamed x9, local copies, waits for them, and re-layouts  4.86 us

profile of v1, /device:TPU:6, one launch (start us, length us, event | category | flops | bytes accessed | tf_op | source)
XLA Modules:
  0.0 74.9 jit_solution(11889503703003504627)
XLA Ops:
  0.0 0.0 copy-start
  0.0 1.6 %copy-done = bf16[4,512,512]{2,1,0:T(8,128)(2,1)S(1)} copy-done((bf16[4,512,512]{2,1,0:T(8,128)(2,1)S(1)}, bf16[4,512,512]{2,1,0:T(8,128)(2,1)}, u32[]{:S(2)}) %copy-start) | copy-done | bytes 2097176
  1.6 0.0 copy-start.1
  1.6 1.1 %copy-done.1 = bf16[32,10240]{1,0:T(8,128)(2,1)S(1)} copy-done((bf16[32,10240]{1,0:T(8,128)(2,1)S(1)}, bf16[32,10240]{1,0:T(8,128)(2,1)}, u32[]{:S(2)}) %copy-start.1) | copy-done | bytes 655384
  2.7 0.0 copy-start.2
  2.7 0.7 copy-done.2
  3.4 0.0 copy-start.3
  3.4 0.7 copy-done.3
  4.0 70.0 %shard_map.46 = bf16[32,10240]{1,0:T(8,128)(2,1)S(1)} custom-call(s32[56]{0:T(128)S(1)} %copy-done.3, bf16[32,10240]{1,0:T(8,128)(2,1)S(1)} %copy-done.1, bf16[4,512,512]{2,1,0:T(8,128)(2,1)S(1)} %copy-done, bf16[4,512]{1,0:T(4,128)(2,1)S(1)} %copy-done.2), custom_call_target="tpu_custom_call" | custom-call | tf_op jit(solution)/shard_map/pallas_call | solution.py:288
  74.1 0.8 %copy.6 = bf16[32,10240]{1,0:T(8,128)(2,1)} copy(bf16[32,10240]{1,0:T(8,128)(2,1)S(1)} %shard_map.46) | data formatting | bytes 1310720
Async XLA Ops:
  0.0 1.6 %copy-start = (bf16[4,512,512]{2,1,0:T(8,128)(2,1)S(1)}, bf16[4,512,512]{2,1,0:T(8,128)(2,1)}, u32[]{:S(2)}) copy-start(bf16[4,512,512]{2,1,0:T(8,128)(2,1)} %panels.1) | copy-start | bytes 6291460
  1.6 1.1 %copy-start.1 = (bf16[32,10240]{1,0:T(8,128)(2,1)S(1)}, bf16[32,10240]{1,0:T(8,128)(2,1)}, u32[]{:S(2)}) copy-start(bf16[32,10240]{1,0:T(8,128)(2,1)} %grads.1) | copy-start | bytes 1966084
  2.7 0.7 copy-start.2
  3.4 0.7 copy-start.3

commit v2 on v1

--- a/solution.py
+++ b/solution.py
@@ -27,8 +27,8 @@
     return jnp.where(k % 2 == 0, k // 2 + 1, 7 - k // 2)
 
 
-def extra_home(e):
-    return (e // 2) * 8 + (e % 2) * 4 + (e // 2) * 2
+def extra_home(e, core):
+    return (e // 2) * 9 + (e % 2) * 4 + core * 2
 
 
 def tile(ref, i):
@@ -36,27 +36,34 @@
 
 
 def kernel(
-    owner, grads, panels, eigs, out,
-    tiles, eig_all, eig_row, eig_mine, stage_s, stage_p, p_buf, s_buf, rx, tx, xs, us,
-    sem_send, sem_t, sem_e, sem_p2, sem_p3, sem_s2, sem_s3, sem_g, sem_o,
+    owner_hbm, grads_hbm, panels_hbm, eigs_hbm, out,
+    owner, grads, panels, eigs,
+    tiles, eig_all, eig_row, eig_mine, eig_f32, eig_out, eig_in,
+    stage_s, stage_x, stage_p, p_buf, s_buf, rx, tx, xs, us,
+    sem_in, sem_send, sem_t, sem_e, sem_p2, sem_p3, sem_p4, sem_x, sem_s2, sem_s3, sem_g, sem_o,
 ):
     r = lax.axis_index("rep")
     w = lax.axis_index("work")
     layer = r // Q
     q = r % Q
+    core = r % 2
+    pair = q - core
+    keeper = 2 * q
     extra = jnp.int32(-1)
     for e in range(EXTRA):
-        extra = jnp.where(w == extra_home(e), e, extra)
+        extra = jnp.where(w == extra_home(e, core), e, extra)
     has_extra = extra >= 0
     mine = jnp.where(has_extra, extra, 0)
 
     barrier = pltpu.get_barrier_semaphore()
 
-    def others(body):
+    def others_z(body):
         @pl.loop(0, 7)
         def _(k):
             body(partner(w, 0, near_first(k)))
 
+    def others(body):
+        others_z(body)
         body(partner(w, 1, 0))
 
         @pl.loop(0, 7)
@@ -87,6 +94,13 @@
 
     def settle(ref, sem):
         pltpu.make_async_copy(ref, ref, sem).wait()
+
+    slab = panels_hbm.at[:, pl.ds(pl.multiple_of(q * 64, 64), 64), :]
+    local(slab, panels, sem_in.at[0])
+    local(eigs_hbm, eigs, sem_in.at[1])
+    local(grads_hbm, grads, sem_in.at[2])
+    local(owner_hbm, owner, sem_in.at[3])
+    settle(eigs, sem_in.at[1])
 
     values = eigs[...].astype(F32)
     for s in range(SLOTS):
@@ -94,19 +108,28 @@
             eig_row[4 * s + c : 4 * s + c + 1, :] = values[s : s + 1, c * 128 : (c + 1) * 128]
     eig_mine[...] = eig_row[...].astype(BF16)
 
+    settle(panels, sem_in.at[0])
+    pltpu.make_async_copy(owner_hbm, owner, sem_in.at[3]).wait()
+    settle(grads, sem_in.at[2])
     pl.semaphore_wait(barrier, W - 1 + Q - 1)
 
     def piece_of(i):
-        rows = pl.multiple_of(q * 64 + (i // 4) * 16, 16)
+        rows = pl.multiple_of((i // 4) * 16, 16)
         return panels.at[:, pl.ds(rows, 16), pl.ds(pl.multiple_of((i % 4) * 128, 128), 128)]
 
     def send_tiles(t):
         remote(piece_of(t), tiles.at[pl.ds(w * SLOTS, SLOTS)], sem_send.at[0], sem_t, work=t)
-        remote(eig_mine, eig_all.at[w], sem_send.at[1], sem_e, work=t)
 
     others(send_tiles)
     local(piece_of(w), tiles.at[pl.ds(w * SLOTS, SLOTS)], sem_t)
-    local(eig_mine, eig_all.at[w], sem_e)
+
+    @pl.when(w == keeper)
+    def _():
+        local(eig_mine, eig_all.at[w], sem_e.at[0])
+
+    @pl.when(w != keeper)
+    def _():
+        remote(eig_mine, eig_all.at[w], sem_send.at[1], sem_e.at[0], work=keeper)
 
     def block_of(j):
         return grads.at[:, pl.ds(pl.multiple_of(j * N, N), N)]
@@ -123,7 +146,7 @@
     @pl.loop(0, EXTRA)
     def _(k):
         e = (k + w) % EXTRA
-        home = extra_home(e)
+        home = extra_home(e, core)
 
         @pl.when(home != w)
         def _():
@@ -148,7 +171,13 @@
     mates(send_p)
     local(stage_p.at[q], p_tile(q), sem_p2)
 
-    @pl.loop(0, RIGHT)
+    @pl.loop(0, EXTRA)
+    def _(e):
+        stage_x[core, e] = tiles[owner[LEFT + layer * RIGHT + W + e]]
+
+    remote(stage_x.at[core], stage_x.at[core], sem_send.at[12], sem_x, rep=layer * Q + pair + 1 - core)
+
+    @pl.loop(0, W)
     def _(j):
         stage_s[j] = tiles[owner[LEFT + layer * RIGHT + j]]
 
@@ -157,19 +186,24 @@
 
     others(send_s)
     local(stage_s.at[w], tile(s_buf.at[0, q], w), sem_s2.at[0])
+
+    settle(stage_x.at[0], sem_x)
+
+    def x_tiles():
+        return s_buf.at[1, pl.ds(pair, 2), w // 4, :, pl.ds(pl.multiple_of((w % 4) * 128, 128), 128)]
 
     @pl.loop(0, EXTRA)
     def _(k):
         e = (k + w) % EXTRA
-        home = extra_home(e)
+        home = extra_home(e, core)
 
         @pl.when(home != w)
         def _():
-            remote(stage_s.at[W + e], tile(s_buf.at[1, q], w), sem_send.at[6], sem_s2.at[1], work=home)
+            remote(stage_x.at[:, e], x_tiles(), sem_send.at[6], sem_s2.at[1], work=home)
 
         @pl.when(home == w)
         def _():
-            local(stage_s.at[W + e], tile(s_buf.at[1, q], w), sem_s2.at[1])
+            local(stage_x.at[:, e], x_tiles(), sem_s2.at[1])
 
     def p_share(k):
         return p_buf.at[:, k // 4, :, pl.ds(pl.multiple_of((k % 4) * 128, 128), 128)]
@@ -177,9 +211,13 @@
     settle(p_share(w), sem_p2)
 
     def send_share(t):
-        remote(p_share(w), p_share(w), sem_send.at[7], sem_p3, work=t)
-
-    others(send_share)
+        remote(p_share(w), p_share(w), sem_send.at[7], sem_p3.at[w % 8], work=t)
+
+    def send_across(k):
+        remote(p_share(k), p_share(k), sem_send.at[13], sem_p4, work=partner(w, 1, 0))
+
+    others_z(send_share)
+    send_across(w)
 
     settle(s_buf.at[0, q], sem_s2.at[0])
 
@@ -190,37 +228,66 @@
 
     @pl.when(has_extra)
     def _():
-        settle(s_buf.at[1, q], sem_s2.at[1])
-
-        def send_slab_extra(m):
-            remote(s_buf.at[1, q], s_buf.at[1, q], sem_send.at[9], sem_s3.at[1], rep=layer * Q + m)
-
-        mates(send_slab_extra)
-
-    settle(eig_all, sem_e)
-
-    def values_of(slot):
-        whole = eig_all[slot // SLOTS].astype(F32)
-        part = slot % SLOTS
-        picked = whole[0:4]
-        for s in range(1, SLOTS):
-            picked = jnp.where(part == s, whole[4 * s : 4 * s + 4], picked)
-        return picked
-
-    left = values_of(owner[r])
+        settle(s_buf.at[1, pl.ds(pair, 2)], sem_s2.at[1])
+
+        @pl.loop(1, 4)
+        def _(k):
+            both = s_buf.at[1, pl.ds(pair, 2)]
+            remote(both, both, sem_send.at[9], sem_s3.at[1], rep=layer * Q + (q + 2 * k) % Q)
+
+    @pl.when(w == keeper)
+    def _():
+        settle(eig_all, sem_e.at[0])
+
+        def values_of(slot):
+            whole = eig_all[slot // SLOTS].astype(F32)
+            part = slot % SLOTS
+            picked = whole[0:4]
+            for s in range(1, SLOTS):
+                picked = jnp.where(part == s, whole[4 * s : 4 * s + 4], picked)
+            return picked
+
+        eig_f32[0:4, :] = values_of(owner[r])
+        eig_f32[12:16, :] = jnp.zeros((4, 128), F32)
+
+        def hand(t):
+            second = jnp.int32(0)
+            for e in range(EXTRA):
+                second = jnp.where(t == extra_home(e, core), e, second)
+            eig_f32[4:8, :] = values_of(owner[LEFT + layer * RIGHT + t])
+            eig_f32[8:12, :] = values_of(owner[LEFT + layer * RIGHT + W + second])
+            eig_out[t] = eig_f32[...].astype(BF16)
+
+        def send_values(t):
+            hand(t)
+            remote(eig_out.at[t], eig_in, sem_send.at[14], sem_e.at[1], work=t)
+
+        others(send_values)
+        hand(w)
+        local(eig_out.at[w], eig_in, sem_e.at[1])
+
+    @pl.loop(0, 7)
+    def _(k):
+        t = partner(w, 0, near_first(k))
+        settle(p_share(t), sem_p3.at[t % 8])
+        send_across(t)
+
+    settle(eig_in, sem_e.at[1])
+    values_in = eig_in[...].astype(F32)
+    left = values_in[0:4]
     columns = []
     for c in range(4):
         columns.append(jnp.transpose(jnp.broadcast_to(left[c : c + 1], (128, 128))))
     left_columns = jnp.concatenate(columns, axis=0)
 
     others_rows = rx.at[0, pl.ds(0, (W - 1) * ROWS), :]
-    settle(others_rows, sem_p3)
+    settle(p_buf.at[:, 0:2], sem_p4)
 
     def out_block(j):
         return out.at[:, pl.ds(pl.multiple_of(j * N, N), N)]
 
     def compute(u, right):
-        settle(s_buf.at[u, 0:7], sem_s3.at[u])
+        settle(s_buf.at[u, 0 : 7 - u], sem_s3.at[u])
         settle(rx.at[u], sem_g.at[u])
         p = p_buf[...].reshape(N, N)
         s = s_buf[u].reshape(N, N)
@@ -240,8 +307,7 @@
             ).astype(BF16)
             tx[u, :, cols] = jnp.dot(p, back, preferred_element_type=F32).astype(BF16)
 
-    right0 = values_of(owner[LEFT + layer * RIGHT + w])
-    compute(0, right0)
+    compute(0, values_in[4:8])
 
     def send_out(t):
         remote(row_slice(tx, 0, t), out_block(w), sem_send.at[10], sem_o, work=t)
@@ -251,8 +317,7 @@
 
     @pl.when(has_extra)
     def _():
-        right1 = values_of(owner[LEFT + layer * RIGHT + W + mine])
-        compute(1, right1)
+        compute(1, values_in[8:12])
 
         def send_out_extra(t):
             remote(row_slice(tx, 1, t), out_block(W + mine), sem_send.at[11], sem_o, work=t)
@@ -261,25 +326,35 @@
         local(row_slice(tx, 1, w), out_block(W + mine), sem_o)
 
     settle(tiles.at[0 : (W - 1) * SLOTS], sem_send.at[0])
-    settle(eig_all.at[0 : W - 1], sem_send.at[1])
+
+    @pl.when(w == keeper)
+    def _():
+        settle(eig_out.at[0 : W - 1], sem_send.at[14])
+
+    @pl.when(w != keeper)
+    def _():
+        settle(eig_mine, sem_send.at[1])
+
     settle(others_rows, sem_send.at[2])
     settle(stage_p.at[0 : Q - 1], sem_send.at[4])
     settle(stage_s.at[0 : W - 1], sem_send.at[5])
-    settle(others_rows, sem_send.at[7])
+    settle(rx.at[0, pl.ds(0, 7 * ROWS), :], sem_send.at[7])
+    settle(stage_x.at[0], sem_send.at[12])
+    settle(p_buf.at[:, 0:2], sem_send.at[13])
     settle(s_buf.at[0, 0:7], sem_send.at[8])
     settle(others_rows, sem_send.at[10])
 
     @pl.when(has_extra)
     def _():
         settle(rx.at[0, pl.ds(0, (EXTRA - 1) * ROWS), :], sem_send.at[3])
-        settle(stage_s.at[0 : EXTRA - 1], sem_send.at[6])
-        settle(s_buf.at[1, 0:7], sem_send.at[9])
+        settle(stage_s.at[0 : 2 * (EXTRA - 1)], sem_send.at[6])
+        settle(s_buf.at[1, 0:6], sem_send.at[9])
         settle(others_rows, sem_send.at[11])
 
     @pl.when(jnp.logical_not(has_extra))
     def _():
         settle(rx.at[0, pl.ds(0, EXTRA * ROWS), :], sem_send.at[3])
-        settle(stage_s.at[0:EXTRA], sem_send.at[6])
+        settle(stage_s.at[0 : 2 * EXTRA], sem_send.at[6])
 
     settle(out, sem_o)
 
@@ -289,18 +364,26 @@
         kernel,
         out_shape=jax.ShapeDtypeStruct(grads.shape, BF16),
         in_specs=[
-            pl.BlockSpec(memory_space=pltpu.SMEM),
-            pl.BlockSpec(memory_space=pl.ANY),
-            pl.BlockSpec(memory_space=pl.ANY),
-            pl.BlockSpec(memory_space=pltpu.VMEM),
+            pl.BlockSpec(memory_space=pltpu.HBM),
+            pl.BlockSpec(memory_space=pltpu.HBM),
+            pl.BlockSpec(memory_space=pltpu.HBM),
+            pl.BlockSpec(memory_space=pltpu.HBM),
         ],
         out_specs=pl.BlockSpec(memory_space=pl.ANY),
         scratch_shapes=[
+            pltpu.SMEM(owner_slot.shape, jnp.int32),
+            pltpu.VMEM(grads.shape, BF16),
+            pltpu.VMEM((SLOTS, N // Q, N), BF16),
+            pltpu.VMEM(eigvals.shape, BF16),
             pltpu.VMEM((W * SLOTS, 16, 128), BF16),
             pltpu.VMEM((W, 16, 128), BF16),
             pltpu.VMEM((16, 128), F32),
             pltpu.VMEM((16, 128), BF16),
-            pltpu.VMEM((RIGHT, 16, 128), BF16),
+            pltpu.VMEM((16, 128), F32),
+            pltpu.VMEM((W, 16, 128), BF16),
+            pltpu.VMEM((16, 128), BF16),
+            pltpu.VMEM((W, 16, 128), BF16),
+            pltpu.VMEM((2, EXTRA, 16, 128), BF16),
             pltpu.VMEM((Q, 16, 128), BF16),
             pltpu.VMEM((Q, 4, 16, N), BF16),
             pltpu.VMEM((2, Q, 4, 16, N), BF16),
@@ -308,9 +391,12 @@
             pltpu.VMEM((2, N, N), BF16),
             pltpu.VMEM((N, N), BF16),
             pltpu.VMEM((N, N), BF16),
-            pltpu.SemaphoreType.DMA((12,)),
+            pltpu.SemaphoreType.DMA((4,)),
+            pltpu.SemaphoreType.DMA((15,)),
             pltpu.SemaphoreType.DMA,
+            pltpu.SemaphoreType.DMA((2,)),
             pltpu.SemaphoreType.DMA,
+            pltpu.SemaphoreType.DMA((8,)),
             pltpu.SemaphoreType.DMA,
             pltpu.SemaphoreType.DMA,
             pltpu.SemaphoreType.DMA((2,)),

time: 75.1 us -> 68.3 us (0.909)
  the two profiles are of different devices: /device:TPU:6 before, /device:TPU:36 now
where the time goes in v2:
time: 68.3 us; the launch traced here: 67.3 us
  Pallas kernels  62.4 us (91%)
  local copies, waits for them, and re-layouts  4.86 us (7%)
    pallas_call x1, Pallas kernels, per_device(): pl.pallas_call(kernel, out_shape=jax.ShapeDtypeStruct(grads.shape, BF16),...  62.4 us
    unnamed x9, local copies, waits for them, and re-layouts  4.86 us

profile of v2, /device:TPU:36, one launch (start us, length us, event | category | flops | bytes accessed | tf_op | source)
XLA Modules:
  0.0 67.3 jit_solution(12795357385623970211)
XLA Ops:
  0.0 0.0 copy-start
  0.0 1.6 %copy-done = bf16[4,512,512]{2,1,0:T(8,128)(2,1)S(1)} copy-done((bf16[4,512,512]{2,1,0:T(8,128)(2,1)S(1)}, bf16[4,512,512]{2,1,0:T(8,128)(2,1)}, u32[]{:S(2)}) %copy-start) | copy-done | bytes 2097176
  1.6 0.0 copy-start.1
  1.6 1.1 %copy-done.1 = bf16[32,10240]{1,0:T(8,128)(2,1)S(1)} copy-done((bf16[32,10240]{1,0:T(8,128)(2,1)S(1)}, bf16[32,10240]{1,0:T(8,128)(2,1)}, u32[]{:S(2)}) %copy-start.1) | copy-done | bytes 655384
  2.7 0.0 copy-start.2
  2.7 0.7 %copy-done.2 = bf16[4,512]{1,0:T(4,128)(2,1)S(1)} copy-done((bf16[4,512]{1,0:T(4,128)(2,1)S(1)}, bf16[4,512]{1,0:T(4,128)(2,1)}, u32[]{:S(2)}) %copy-start.2) | copy-done | bytes 4120
  3.4 0.0 copy-start.3
  3.4 0.7 copy-done.3
  4.0 62.4 %shard_map.46 = bf16[32,10240]{1,0:T(8,128)(2,1)S(1)} custom-call(s32[56]{0:T(128)S(1)} %copy-done.3, bf16[32,10240]{1,0:T(8,128)(2,1)S(1)} %copy-done.1, bf16[4,512,512]{2,1,0:T(8,128)(2,1)S(1)} %copy-done, bf16[4,512]{1,0:T(4,128)(2,1)S(1)} %copy-done.2), custom_call_target="tpu_custom_call" | custom-call | tf_op jit(solution)/shard_map/pallas_call | solution.py:363
  66.5 0.8 %copy.6 = bf16[32,10240]{1,0:T(8,128)(2,1)} copy(bf16[32,10240]{1,0:T(8,128)(2,1)S(1)} %shard_map.46) | data formatting | bytes 1310720
Async XLA Ops:
  0.0 1.6 %copy-start = (bf16[4,512,512]{2,1,0:T(8,128)(2,1)S(1)}, bf16[4,512,512]{2,1,0:T(8,128)(2,1)}, u32[]{:S(2)}) copy-start(bf16[4,512,512]{2,1,0:T(8,128)(2,1)} %panels_hbm.1) | copy-start | bytes 6291460
  1.6 1.1 %copy-start.1 = (bf16[32,10240]{1,0:T(8,128)(2,1)S(1)}, bf16[32,10240]{1,0:T(8,128)(2,1)}, u32[]{:S(2)}) copy-start(bf16[32,10240]{1,0:T(8,128)(2,1)} %grads_hbm.1) | copy-start | bytes 1966084
  2.7 0.7 %copy-start.2 = (bf16[4,512]{1,0:T(4,128)(2,1)S(1)}, bf16[4,512]{1,0:T(4,128)(2,1)}, u32[]{:S(2)}) copy-start(bf16[4,512]{1,0:T(4,128)(2,1)} %eigs_hbm.1) | copy-start | bytes 12292
  3.4 0.7 copy-start.3

commit v3 on v2

v3 whole, which is shorter than its diff:
```python
import jax
import jax.numpy as jnp
from jax import lax
from jax.experimental import pallas as pl
from jax.experimental.pallas import tpu as pltpu
from jax.sharding import PartitionSpec as P

MESH = pl.DeviceIdType.MESH
N = 512
W = 16
Q = 8
ROWS = 32
RIGHT = 20
LEFT = 16
SLOTS = 4
EXTRA = RIGHT - W
DAMPING = 0.2
BF16 = jnp.bfloat16
F32 = jnp.float32


def partner(w, dx, dz):
    return ((w // 8 + dx) % 2) * 8 + (w % 8 + dz) % 8


def near_first(k):
    return jnp.where(k % 2 == 0, k // 2 + 1, 7 - k // 2)


def extra_home(e, core):
    return (e // 2) * 9 + (e % 2) * 4 + core * 2


def tile(ref, i):
    return ref.at[i // 4, :, pl.ds(pl.multiple_of((i % 4) * 128, 128), 128)]


def kernel(
    owner_hbm, grads_hbm, panels_hbm, eigs_hbm, out,
    owner, grads, panels, eigs,
    tiles, eig_all, eig_mine, eig_f32, eig_out, eig_in,
    stage_s, stage_x, stage_p, p_buf, s_buf, rx, tx, xs, us,
    sem_in, sem_send, sem_t, sem_e, sem_p2, sem_p3, sem_p4, sem_x, sem_s2, sem_s3, sem_g, sem_o,
):
    r = lax.axis_index("rep")
    w = lax.axis_index("work")
    layer = r // Q
    q = r % Q
    core = r % 2
    pair = q - core
    keeper = 2 * q
    extra = jnp.int32(-1)
    for e in range(EXTRA):
        extra = jnp.where(w == extra_home(e, core), e, extra)
    has_extra = extra >= 0
    mine = jnp.where(has_extra, extra, 0)

    barrier = pltpu.get_barrier_semaphore()

    def others_z(body):
        @pl.loop(0, 7)
        def _(k):
            body(partner(w, 0, near_first(k)))

    def others_x(body):
        @pl.loop(0, 7)
        def _(k):
            body(partner(w, 1, near_first(k)))

    def others(body):
        others_z(body)
        body(partner(w, 1, 0))
        others_x(body)

    def mates(body):
        @pl.loop(1, Q)
        def _(k):
            body((q + k) % Q)

    def greet(t):
        pl.semaphore_signal(barrier, inc=1, device_id={"work": t}, device_id_type=MESH)

    def greet_mate(m):
        pl.semaphore_signal(barrier, inc=1, device_id={"rep": layer * Q + m}, device_id_type=MESH)

    others(greet)
    mates(greet_mate)

    def remote(src, dst, send, recv, **where):
        pltpu.make_async_remote_copy(
            src_ref=src, dst_ref=dst, send_sem=send, recv_sem=recv, device_id=where, device_id_type=MESH
        ).start()

    def local(src, dst, sem):
        pltpu.make_async_copy(src, dst, sem).start()

    def settle(ref, sem):
        pltpu.make_async_copy(ref, ref, sem).wait()

    slab = panels_hbm.at[:, pl.ds(pl.multiple_of(q * 64, 64), 64), :]
    local(slab, panels, sem_in.at[0])
    local(eigs_hbm, eigs, sem_in.at[1])
    local(grads_hbm, grads, sem_in.at[2])
    local(owner_hbm, owner, sem_in.at[3])
    settle(panels, sem_in.at[0])
    pl.semaphore_wait(barrier, W - 1 + Q - 1)

    def piece_of(i):
        rows = pl.multiple_of((i // 4) * 16, 16)
        return panels.at[:, pl.ds(rows, 16), pl.ds(pl.multiple_of((i % 4) * 128, 128), 128)]

    def tiles_out():
        def send_tiles(t):
            remote(piece_of(t), tiles.at[pl.ds(w * SLOTS, SLOTS)], sem_send.at[0], sem_t, work=t)

        others(send_tiles)
        local(piece_of(w), tiles.at[pl.ds(w * SLOTS, SLOTS)], sem_t)

    def values_out():
        settle(eigs, sem_in.at[1])

        values = eigs[...].astype(F32)
        for s in range(SLOTS):
            for c in range(4):
                eig_f32[c : c + 1, :] = values[s : s + 1, c * 128 : (c + 1) * 128]
            eig_mine[s] = eig_f32[...].astype(BF16)

        @pl.when(w == keeper)
        def _():
            local(eig_mine, eig_all.at[pl.ds(w * SLOTS, SLOTS)], sem_e.at[0])

        @pl.when(w != keeper)
        def _():
            remote(eig_mine, eig_all.at[pl.ds(w * SLOTS, SLOTS)], sem_send.at[1], sem_e.at[0], work=keeper)

    def block_of(j):
        return grads.at[:, pl.ds(pl.multiple_of(j * N, N), N)]

    def row_slice(ref, u, k):
        return ref.at[u, pl.ds(pl.multiple_of(k * ROWS, ROWS), ROWS), :]

    def send_rows(t):
        remote(block_of(t), row_slice(rx, 0, w), sem_send.at[2], sem_g.at[0], work=t)

    def rows_ready():
        settle(grads, sem_in.at[2])
        rows_own()

    def rows_own():
        local(block_of(w), row_slice(rx, 0, w), sem_g.at[0])

    def rows_to(dx, *steps):
        for dz in steps:
            send_rows(partner(w, dx, dz))

    def rows_extra(a, b):
        @pl.loop(a, b)
        def _(k):
            e = (k + w) % EXTRA
            home = extra_home(e, core)

            @pl.when(home != w)
            def _():
                remote(block_of(W + e), row_slice(rx, 1, w), sem_send.at[3], sem_g.at[1], work=home)

            @pl.when(home == w)
            def _():
                local(block_of(W + e), row_slice(rx, 1, w), sem_g.at[1])

    def p_tile(k):
        return tile(p_buf.at[k], w)

    def left_tiles():
        settle(tiles, sem_t)
        pltpu.make_async_copy(owner_hbm, owner, sem_in.at[3]).wait()

        @pl.loop(0, Q)
        def _(m):
            stage_p[m] = tiles[owner[layer * Q + m]]

        def send_p(m):
            remote(stage_p.at[m], p_tile(q), sem_send.at[4], sem_p2, rep=layer * Q + m)

        mates(send_p)
        local(stage_p.at[q], p_tile(q), sem_p2)

    def extra_tiles_pair():
        @pl.loop(0, EXTRA)
        def _(e):
            stage_x[core, e] = tiles[owner[LEFT + layer * RIGHT + W + e]]

        remote(stage_x.at[core], stage_x.at[core], sem_send.at[12], sem_x, rep=layer * Q + pair + 1 - core)

    def right_tiles():
        @pl.loop(0, W)
        def _(j):
            stage_s[j] = tiles[owner[LEFT + layer * RIGHT + j]]

        def send_s(t):
            remote(stage_s.at[t], tile(s_buf.at[0, q], w), sem_send.at[5], sem_s2.at[0], work=t)

        others(send_s)
        local(stage_s.at[w], tile(s_buf.at[0, q], w), sem_s2.at[0])

    def extra_tiles():
        settle(stage_x.at[0], sem_x)

        def x_tiles():
            return s_buf.at[1, pl.ds(pair, 2), w // 4, :, pl.ds(pl.multiple_of((w % 4) * 128, 128), 128)]

        @pl.loop(0, EXTRA)
        def _(k):
            e = (k + w) % EXTRA
            home = extra_home(e, core)

            @pl.when(home != w)
            def _():
                remote(stage_x.at[:, e], x_tiles(), sem_send.at[6], sem_s2.at[1], work=home)

            @pl.when(home == w)
            def _():
                local(stage_x.at[:, e], x_tiles(), sem_s2.at[1])

    def p_share(k):
        return p_buf.at[:, k // 4, :, pl.ds(pl.multiple_of((k % 4) * 128, 128), 128)]

    def send_across(k):
        remote(p_share(k), p_share(k), sem_send.at[13], sem_p4, work=partner(w, 1, 0))

    def left_shares():
        settle(p_share(w), sem_p2)

        def send_share(t):
            remote(p_share(w), p_share(w), sem_send.at[7], sem_p3.at[w % 8], work=t)

        others_z(send_share)
        send_across(w)

    def right_slabs():
        settle(s_buf.at[0, q], sem_s2.at[0])

        def send_slab(m):
            remote(s_buf.at[0, q], s_buf.at[0, q], sem_send.at[8], sem_s3.at[0], rep=layer * Q + m)

        mates(send_slab)

    def extra_slabs():
        @pl.when(has_extra)
        def _():
            settle(s_buf.at[1, pl.ds(pair, 2)], sem_s2.at[1])

            @pl.loop(1, 4)
            def _(k):
                both = s_buf.at[1, pl.ds(pair, 2)]
                remote(both, both, sem_send.at[9], sem_s3.at[1], rep=layer * Q + (q + 2 * k) % Q)

    def hand_values():
        @pl.when(w == keeper)
        def _():
            settle(eig_all, sem_e.at[0])

            def hand(t):
                second = jnp.int32(0)
                for e in range(EXTRA):
                    second = jnp.where(t == extra_home(e, core), e, second)
                eig_out[t, 0] = eig_all[owner[r]]
                eig_out[t, 1] = eig_all[owner[LEFT + layer * RIGHT + t]]
                eig_out[t, 2] = eig_all[owner[LEFT + layer * RIGHT + W + second]]

            def send_values(t):
                hand(t)
                remote(eig_out.at[t], eig_in, sem_send.at[14], sem_e.at[1], work=t)

            others(send_values)
            hand(w)
            local(eig_out.at[w], eig_in, sem_e.at[1])

    def pass_on():
        @pl.loop(0, 7)
        def _(k):
            t = partner(w, 0, near_first(k))
            settle(p_share(t), sem_p3.at[t % 8])
            send_across(t)

    tiles_out()
    rows_ready()
    rows_extra(0, 4)

    @pl.when(core == 0)
    def _():
        rows_to(1, 0)
        rows_to(1, 1, 7)
        rows_to(1, 2, 6)
        rows_to(1, 3, 5)
        rows_to(1, 4)
        rows_to(0, 1, 7)
        rows_to(0, 2, 6)
        rows_to(0, 3, 5)
        rows_to(0, 4)

    values_out()
    left_tiles()
    extra_tiles_pair()
    right_tiles()
    extra_tiles()
    left_shares()
    right_slabs()
    extra_slabs()
    hand_values()

    @pl.when(core == 1)
    def _():
        rows_to(1, 0)
        rows_to(1, 1, 7)
        rows_to(1, 2, 6)
        rows_to(1, 3, 5)
        rows_to(1, 4)
        rows_to(0, 1, 7)
        rows_to(0, 2, 6)
        rows_to(0, 3, 5)
        rows_to(0, 4)

    pass_on()

    settle(eig_in, sem_e.at[1])
    left = eig_in[0].astype(F32)
    columns = []
    for c in range(4):
        columns.append(jnp.transpose(jnp.broadcast_to(left[c : c + 1], (128, 128))))
    left_columns = jnp.concatenate(columns, axis=0)

    others_rows = rx.at[0, pl.ds(0, (W - 1) * ROWS), :]
    settle(p_buf.at[:, 0:2], sem_p4)

    def compute(u, j):
        settle(rx.at[u], sem_g.at[u])
        p = p_buf[...].reshape(N, N)
        halves = [slice(c * 256, (c + 1) * 256) for c in range(2)]
        for cols in halves:
            xs[:, cols] = lax.dot_general(
                p, rx[u, :, cols], (((0,), (0,)), ((), ())), preferred_element_type=F32
            ).astype(BF16)
        settle(s_buf.at[u, 0 : 7 - u], sem_s3.at[u])
        s = s_buf[u].reshape(N, N)
        right = eig_in[1 + u].astype(F32)
        for c in range(4):
            cols = slice(c * 128, (c + 1) * 128)
            turned = jnp.dot(xs[...], s[:, cols], preferred_element_type=F32)
            us[:, cols] = (turned / (left_columns * right[c : c + 1] + DAMPING)).astype(BF16)
        for c, cols in enumerate(halves):
            back = lax.dot_general(
                us[...], s[cols], (((1,), (1,)), ((), ())), preferred_element_type=F32
            ).astype(BF16)
            tx[u, c] = jnp.dot(p, back, preferred_element_type=F32).astype(BF16)

            def send_out(t):
                remote(own_rows(t), out_block(t), sem_send.at[10 + u], sem_o, work=t)

            def own_rows(t):
                return tx.at[u, c, pl.ds(pl.multiple_of(t * ROWS, ROWS), ROWS), :]

            def out_block(t):
                return out.at[:, pl.ds(pl.multiple_of(j * N + c * 256, 256), 256)]

            others(send_out)
            local(own_rows(w), out_block(w), sem_o)

    compute(0, w)

    @pl.when(has_extra)
    def _():
        compute(1, W + mine)

    settle(tiles.at[0 : (W - 1) * SLOTS], sem_send.at[0])

    @pl.when(w == keeper)
    def _():
        settle(eig_out.at[0 : W - 1], sem_send.at[14])

    @pl.when(w != keeper)
    def _():
        settle(eig_mine, sem_send.at[1])

    settle(stage_p.at[0 : Q - 1], sem_send.at[4])
    settle(stage_s.at[0 : W - 1], sem_send.at[5])
    settle(rx.at[0, pl.ds(0, 7 * ROWS), :], sem_send.at[7])
    settle(stage_x.at[0], sem_send.at[12])
    settle(p_buf.at[:, 0:2], sem_send.at[13])
    settle(s_buf.at[0, 0:7], sem_send.at[8])
    settle(others_rows, sem_send.at[2])
    settle(others_rows, sem_send.at[10])

    @pl.when(has_extra)
    def _():
        settle(rx.at[0, pl.ds(0, (EXTRA - 1) * ROWS), :], sem_send.at[3])
        settle(stage_s.at[0 : 2 * (EXTRA - 1)], sem_send.at[6])
        settle(s_buf.at[1, 0:6], sem_send.at[9])
        settle(others_rows, sem_send.at[11])

    @pl.when(jnp.logical_not(has_extra))
    def _():
        settle(rx.at[0, pl.ds(0, EXTRA * ROWS), :], sem_send.at[3])
        settle(stage_s.at[0 : 2 * EXTRA], sem_send.at[6])

    settle(out, sem_o)


def per_device(grads, panels, eigvals, owner_slot):
    return pl.pallas_call(
        kernel,
        out_shape=jax.ShapeDtypeStruct(grads.shape, BF16),
        in_specs=[
            pl.BlockSpec(memory_space=pltpu.HBM),
            pl.BlockSpec(memory_space=pltpu.HBM),
            pl.BlockSpec(memory_space=pltpu.HBM),
            pl.BlockSpec(memory_space=pltpu.HBM),
        ],
        out_specs=pl.BlockSpec(memory_space=pl.ANY),
        scratch_shapes=[
            pltpu.SMEM(owner_slot.shape, jnp.int32),
            pltpu.VMEM(grads.shape, BF16),
            pltpu.VMEM((SLOTS, N // Q, N), BF16),
            pltpu.VMEM(eigvals.shape, BF16),
            pltpu.VMEM((W * SLOTS, 16, 128), BF16),
            pltpu.VMEM((W * SLOTS, 16, 128), BF16),
            pltpu.VMEM((SLOTS, 16, 128), BF16),
            pltpu.VMEM((16, 128), F32),
            pltpu.VMEM((W, 3, 16, 128), BF16),
            pltpu.VMEM((3, 16, 128), BF16),
            pltpu.VMEM((W, 16, 128), BF16),
            pltpu.VMEM((2, EXTRA, 16, 128), BF16),
            pltpu.VMEM((Q, 16, 128), BF16),
            pltpu.VMEM((Q, 4, 16, N), BF16),
            pltpu.VMEM((2, Q, 4, 16, N), BF16),
            pltpu.VMEM((2, N, N), BF16),
            pltpu.VMEM((2, 2, N, N // 2), BF16),
            pltpu.VMEM((N, N), BF16),
            pltpu.VMEM((N, N), BF16),
            pltpu.SemaphoreType.DMA((4,)),
            pltpu.SemaphoreType.DMA((15,)),
            pltpu.SemaphoreType.DMA,
            pltpu.SemaphoreType.DMA((2,)),
            pltpu.SemaphoreType.DMA,
            pltpu.SemaphoreType.DMA((8,)),
            pltpu.SemaphoreType.DMA,
            pltpu.SemaphoreType.DMA,
            pltpu.SemaphoreType.DMA((2,)),
            pltpu.SemaphoreType.DMA((2,)),
            pltpu.SemaphoreType.DMA((2,)),
            pltpu.SemaphoreType.DMA,
        ],
        compiler_params=pltpu.CompilerParams(
            collective_id=0, has_side_effects=True, vmem_limit_bytes=32 * 1024 * 1024
        ),
    )(*[pltpu.with_memory_space_constraint(x, pltpu.HBM) for x in (owner_slot, grads, panels, eigvals)])


def solution(mesh):
    return jax.shard_map(
        per_device,
        mesh=mesh,
        in_specs=(P(("rep", "work"), None), P("work", None, None), P("work", None), P()),
        out_specs=P(("rep", "work"), None),
        check_vma=False,
    )
```

time: 68.3 us -> 61.1 us (0.89); the launches traced: 67.3 us -> 60.9 us
  local copies, waits for them, and re-layouts: 4.86 us -> 0.84 us
  Pallas kernels: 62.4 us -> 60 us
    unnamed x9 -> x1, local copies, waits for them, and re-layouts: 4.86 us -> 0.84 us
    pallas_call x1, Pallas kernels: 62.4 us -> 60 us  [per_device(): pl.pallas_call(kernel, out_shape=jax.ShapeDtypeStruct(grads.shape, BF16),...]
where the time goes in v3:
time: 61.1 us; the launch traced here: 60.9 us
  Pallas kernels  60 us (98%)
  local copies, waits for them, and re-layouts  0.84 us (1%)
    pallas_call x1, Pallas kernels, per_device(): pl.pallas_call(kernel, out_shape=jax.ShapeDtypeStruct(grads.shape, BF16),...  60 us

profile of v3, /device:TPU:36, one launch (start us, length us, event | category | flops | bytes accessed | tf_op | source)
XLA Modules:
  0.0 60.9 jit_solution(9244339934619452357)
XLA Ops:
  0.0 60.0 %shard_map.46 = bf16[32,10240]{1,0:T(8,128)(2,1)S(1)} custom-call(s32[56]{0:T(128)} %owner_hbm.1, bf16[32,10240]{1,0:T(8,128)(2,1)} %grads_hbm.1, bf16[4,512,512]{2,1,0:T(8,128)(2,1)} %panels_hbm.1, bf16[4,512]{1,0:T(4,128)(2,1)} %eigs_hbm.1), custom_call_target="tpu_custom_call" | custom-call | tf_op jit(solution)/shard_map/pallas_call | solution.py:409
  60.0 0.8 %copy.6 = bf16[32,10240]{1,0:T(8,128)(2,1)} copy(bf16[32,10240]{1,0:T(8,128)(2,1)S(1)} %shard_map.46) | data formatting | bytes 1310720

commit v4 on v3

--- a/solution.py
+++ b/solution.py
@@ -284,7 +284,6 @@
 
     tiles_out()
     rows_ready()
-    rows_extra(0, 4)
 
     @pl.when(core == 0)
     def _():
@@ -305,7 +304,6 @@
     extra_tiles()
     left_shares()
     right_slabs()
-    extra_slabs()
     hand_values()
 
     @pl.when(core == 1)
@@ -321,6 +319,8 @@
         rows_to(0, 4)
 
     pass_on()
+    rows_extra(0, 4)
+    extra_slabs()
 
     settle(eig_in, sem_e.at[1])
     left = eig_in[0].astype(F32)

time: 61.1 us -> 59.1 us (0.967)
  Pallas kernels: 60 us -> 57.5 us
    pallas_call x1, Pallas kernels: 60 us -> 57.5 us  [per_device(): pl.pallas_call(kernel, out_shape=jax.ShapeDtypeStruct(grads.shape, BF16),...]
where the time goes in v4:
time: 59.1 us; the launch traced here: 58.3 us
  Pallas kernels  57.5 us (97%)
  local copies, waits for them, and re-layouts  0.84 us (1%)
    pallas_call x1, Pallas kernels, per_device(): pl.pallas_call(kernel, out_shape=jax.ShapeDtypeStruct(grads.shape, BF16),...  57.5 us

profile of v4, /device:TPU:36, one launch (start us, length us, event | category | flops | bytes accessed | tf_op | source)
XLA Modules:
  0.0 58.3 jit_solution(16359296758227405762)
XLA Ops:
  0.0 57.5 %shard_map.46 = bf16[32,10240]{1,0:T(8,128)(2,1)S(1)} custom-call(s32[56]{0:T(128)} %owner_hbm.1, bf16[32,10240]{1,0:T(8,128)(2,1)} %grads_hbm.1, bf16[4,512,512]{2,1,0:T(8,128)(2,1)} %panels_hbm.1, bf16[4,512]{1,0:T(4,128)(2,1)} %eigs_hbm.1), custom_call_target="tpu_custom_call" | custom-call | tf_op jit(solution)/shard_map/pallas_call | solution.py:409
  57.5 0.8 %copy.6 = bf16[32,10240]{1,0:T(8,128)(2,1)} copy(bf16[32,10240]{1,0:T(8,128)(2,1)S(1)} %shard_map.46) | data formatting | bytes 1310720

commit v5 on v4

--- a/solution.py
+++ b/solution.py
@@ -38,7 +38,7 @@
 def kernel(
     owner_hbm, grads_hbm, panels_hbm, eigs_hbm, out,
     owner, grads, panels, eigs,
-    tiles, eig_all, eig_mine, eig_f32, eig_out, eig_in,
+    tiles, eig_all, eig_mine, eig_f32, eig_slot, eig_out, eig_in,
     stage_s, stage_x, stage_p, p_buf, s_buf, rx, tx, xs, us,
     sem_in, sem_send, sem_t, sem_e, sem_p2, sem_p3, sem_p4, sem_x, sem_s2, sem_s3, sem_g, sem_o,
 ):
@@ -122,16 +122,16 @@
         values = eigs[...].astype(F32)
         for s in range(SLOTS):
             for c in range(4):
-                eig_f32[c : c + 1, :] = values[s : s + 1, c * 128 : (c + 1) * 128]
-            eig_mine[s] = eig_f32[...].astype(BF16)
+                eig_f32[4 * s + c : 4 * s + c + 1, :] = values[s : s + 1, c * 128 : (c + 1) * 128]
+        eig_mine[...] = eig_f32[...].astype(BF16)
 
         @pl.when(w == keeper)
         def _():
-            local(eig_mine, eig_all.at[pl.ds(w * SLOTS, SLOTS)], sem_e.at[0])
+            local(eig_mine, eig_all.at[w], sem_e.at[0])
 
         @pl.when(w != keeper)
         def _():
-            remote(eig_mine, eig_all.at[pl.ds(w * SLOTS, SLOTS)], sem_send.at[1], sem_e.at[0], work=keeper)
+            remote(eig_mine, eig_all.at[w], sem_send.at[1], sem_e.at[0], work=keeper)
 
     def block_of(j):
         return grads.at[:, pl.ds(pl.multiple_of(j * N, N), N)]
@@ -259,13 +259,20 @@
         def _():
             settle(eig_all, sem_e.at[0])
 
+            for k in range(W):
+                rows = eig_all[k].astype(F32)
+                for s in range(SLOTS):
+                    eig_slot[k * SLOTS + s, 0:4, :] = rows[4 * s : 4 * s + 4]
+
+            eig_f32[0:4, :] = eig_slot[owner[r], 0:4, :]
+
             def hand(t):
                 second = jnp.int32(0)
                 for e in range(EXTRA):
                     second = jnp.where(t == extra_home(e, core), e, second)
-                eig_out[t, 0] = eig_all[owner[r]]
-                eig_out[t, 1] = eig_all[owner[LEFT + layer * RIGHT + t]]
-                eig_out[t, 2] = eig_all[owner[LEFT + layer * RIGHT + W + second]]
+                eig_f32[4:8, :] = eig_slot[owner[LEFT + layer * RIGHT + t], 0:4, :]
+                eig_f32[8:12, :] = eig_slot[owner[LEFT + layer * RIGHT + W + second], 0:4, :]
+                eig_out[t] = eig_f32[...].astype(BF16)
 
             def send_values(t):
                 hand(t)
@@ -303,8 +310,8 @@
     right_tiles()
     extra_tiles()
     left_shares()
+    hand_values()
     right_slabs()
-    hand_values()
 
     @pl.when(core == 1)
     def _():
@@ -323,7 +330,8 @@
     extra_slabs()
 
     settle(eig_in, sem_e.at[1])
-    left = eig_in[0].astype(F32)
+    values_in = eig_in[...].astype(F32)
+    left = values_in[0:4]
     columns = []
     for c in range(4):
         columns.append(jnp.transpose(jnp.broadcast_to(left[c : c + 1], (128, 128))))
@@ -342,11 +350,11 @@
             ).astype(BF16)
         settle(s_buf.at[u, 0 : 7 - u], sem_s3.at[u])
         s = s_buf[u].reshape(N, N)
-        right = eig_in[1 + u].astype(F32)
-        for c in range(4):
-            cols = slice(c * 128, (c + 1) * 128)
+        right = values_in[4 + 4 * u : 8 + 4 * u]
+        for c, cols in enumerate(halves):
             turned = jnp.dot(xs[...], s[:, cols], preferred_element_type=F32)
-            us[:, cols] = (turned / (left_columns * right[c : c + 1] + DAMPING)).astype(BF16)
+            outer = [left_columns * right[k : k + 1] for k in (2 * c, 2 * c + 1)]
+            us[:, cols] = (turned / (jnp.concatenate(outer, axis=1) + DAMPING)).astype(BF16)
         for c, cols in enumerate(halves):
             back = lax.dot_general(
                 us[...], s[cols], (((1,), (1,)), ((), ())), preferred_element_type=F32
@@ -422,11 +430,12 @@
             pltpu.VMEM((SLOTS, N // Q, N), BF16),
             pltpu.VMEM(eigvals.shape, BF16),
             pltpu.VMEM((W * SLOTS, 16, 128), BF16),
-            pltpu.VMEM((W * SLOTS, 16, 128), BF16),
-            pltpu.VMEM((SLOTS, 16, 128), BF16),
+            pltpu.VMEM((W, 16, 128), BF16),
+            pltpu.VMEM((16, 128), BF16),
             pltpu.VMEM((16, 128), F32),
-            pltpu.VMEM((W, 3, 16, 128), BF16),
-            pltpu.VMEM((3, 16, 128), BF16),
+            pltpu.VMEM((W * SLOTS, 8, 128), F32),
+            pltpu.VMEM((W, 16, 128), BF16),
+            pltpu.VMEM((16, 128), BF16),
             pltpu.VMEM((W, 16, 128), BF16),
             pltpu.VMEM((2, EXTRA, 16, 128), BF16),
             pltpu.VMEM((Q, 16, 128), BF16),

time: 59.1 us -> 57.8 us (0.978)
  Pallas kernels: 57.5 us -> 56 us
    pallas_call x1, Pallas kernels: 57.5 us -> 56 us  [per_device(): pl.pallas_call(kernel, out_shape=jax.ShapeDtypeStruct(grads.shape, BF16),...]
where the time goes in v5:
time: 57.8 us; the launch traced here: 56.8 us
  Pallas kernels  56 us (97%)
  local copies, waits for them, and re-layouts  0.84 us (1%)
    pallas_call x1, Pallas kernels, per_device(): pl.pallas_call(kernel, out_shape=jax.ShapeDtypeStruct(grads.shape, BF16),...  56 us

profile of v5, /device:TPU:36, one launch (start us, length us, event | category | flops | bytes accessed | tf_op | source)
XLA Modules:
  0.0 56.8 jit_solution(4433262421385559939)
XLA Ops:
  0.0 56.0 %shard_map.46 = bf16[32,10240]{1,0:T(8,128)(2,1)S(1)} custom-call(s32[56]{0:T(128)} %owner_hbm.1, bf16[32,10240]{1,0:T(8,128)(2,1)} %grads_hbm.1, bf16[4,512,512]{2,1,0:T(8,128)(2,1)} %panels_hbm.1, bf16[4,512]{1,0:T(4,128)(2,1)} %eigs_hbm.1), custom_call_target="tpu_custom_call" | custom-call | tf_op jit(solution)/shard_map/pallas_call | solution.py:417
  56.0 0.8 %copy.6 = bf16[32,10240]{1,0:T(8,128)(2,1)} copy(bf16[32,10240]{1,0:T(8,128)(2,1)S(1)} %shard_map.46) | data formatting | bytes 1310720

commit v6 on v5

--- a/solution.py
+++ b/solution.py
@@ -83,7 +83,10 @@
     def greet_mate(m):
         pl.semaphore_signal(barrier, inc=1, device_id={"rep": layer * Q + m}, device_id_type=MESH)
 
-    others(greet)
+    for dz in (4, 3, 5, 2, 6, 1, 7, 0):
+        greet(partner(w, 1, dz))
+        if dz:
+            greet(partner(w, 0, dz))
     mates(greet_mate)
 
     def remote(src, dst, send, recv, **where):
@@ -113,7 +116,11 @@
         def send_tiles(t):
             remote(piece_of(t), tiles.at[pl.ds(w * SLOTS, SLOTS)], sem_send.at[0], sem_t, work=t)
 
-        others(send_tiles)
+        for dz in (1, 7, 2, 6, 3, 5, 4):
+            send_tiles(partner(w, 0, dz))
+        send_tiles(partner(w, 1, 0))
+        for dz in (4, 3, 5, 2, 6, 1, 7):
+            send_tiles(partner(w, 1, dz))
         local(piece_of(w), tiles.at[pl.ds(w * SLOTS, SLOTS)], sem_t)
 
     def values_out():
@@ -326,8 +333,8 @@
         rows_to(0, 4)
 
     pass_on()
+    extra_slabs()
     rows_extra(0, 4)
-    extra_slabs()
 
     settle(eig_in, sem_e.at[1])
     values_in = eig_in[...].astype(F32)
@@ -356,10 +363,10 @@
             outer = [left_columns * right[k : k + 1] for k in (2 * c, 2 * c + 1)]
             us[:, cols] = (turned / (jnp.concatenate(outer, axis=1) + DAMPING)).astype(BF16)
         for c, cols in enumerate(halves):
-            back = lax.dot_general(
+            xs[:, cols] = lax.dot_general(
                 us[...], s[cols], (((1,), (1,)), ((), ())), preferred_element_type=F32
             ).astype(BF16)
-            tx[u, c] = jnp.dot(p, back, preferred_element_type=F32).astype(BF16)
+            tx[u, c] = jnp.dot(p, xs[:, cols], preferred_element_type=F32).astype(BF16)
 
             def send_out(t):
                 remote(own_rows(t), out_block(t), sem_send.at[10 + u], sem_o, work=t)

time: 57.8 us -> 56.9 us (0.984); the launches traced: 56.8 us -> 56.7 us
  no operation moved by 1% of the time
where the time goes in v6:
time: 56.9 us; the launch traced here: 56.7 us
  Pallas kernels  55.9 us (98%)
  local copies, waits for them, and re-layouts  0.84 us (1%)
    pallas_call x1, Pallas kernels, per_device(): pl.pallas_call(kernel, out_shape=jax.ShapeDtypeStruct(grads.shape, BF16),...  55.9 us

profile of v6, /device:TPU:36, one launch (start us, length us, event | category | flops | bytes accessed | tf_op | source)
XLA Modules:
  0.0 56.7 jit_solution(10423761033163586522)
XLA Ops:
  0.0 55.9 %shard_map.46 = bf16[32,10240]{1,0:T(8,128)(2,1)S(1)} custom-call(s32[56]{0:T(128)} %owner_hbm.1, bf16[32,10240]{1,0:T(8,128)(2,1)} %grads_hbm.1, bf16[4,512,512]{2,1,0:T(8,128)(2,1)} %panels_hbm.1, bf16[4,512]{1,0:T(4,128)(2,1)} %eigs_hbm.1), custom_call_target="tpu_custom_call" | custom-call | tf_op jit(solution)/shard_map/pallas_call | solution.py:424
  55.9 0.8 %copy.6 = bf16[32,10240]{1,0:T(8,128)(2,1)} copy(bf16[32,10240]{1,0:T(8,128)(2,1)S(1)} %shard_map.46) | data formatting | bytes 1310720

commit v7 on v6

--- a/solution.py
+++ b/solution.py
@@ -206,7 +206,10 @@
         def send_s(t):
             remote(stage_s.at[t], tile(s_buf.at[0, q], w), sem_send.at[5], sem_s2.at[0], work=t)
 
-        others(send_s)
+        others_z(send_s)
+        send_s(partner(w, 1, 0))
+        for dz in (4, 3, 5, 2, 6, 1, 7):
+            send_s(partner(w, 1, dz))
         local(stage_s.at[w], tile(s_buf.at[0, q], w), sem_s2.at[0])
 
     def extra_tiles():

time: 56.9 us -> 56.9 us (level)
  no operation moved by 1% of the time
where the time goes in v7:
time: 56.9 us; the launch traced here: 56.8 us
  Pallas kernels  55.9 us (98%)
  local copies, waits for them, and re-layouts  0.84 us (1%)
    pallas_call x1, Pallas kernels, per_device(): pl.pallas_call(kernel, out_shape=jax.ShapeDtypeStruct(grads.shape, BF16),...  55.9 us

profile of v7, /device:TPU:36, one launch (start us, length us, event | category | flops | bytes accessed | tf_op | source)
XLA Modules:
  0.0 56.8 jit_solution(4502336052533252341)
XLA Ops:
  0.0 55.9 %shard_map.46 = bf16[32,10240]{1,0:T(8,128)(2,1)S(1)} custom-call(s32[56]{0:T(128)} %owner_hbm.1, bf16[32,10240]{1,0:T(8,128)(2,1)} %grads_hbm.1, bf16[4,512,512]{2,1,0:T(8,128)(2,1)} %panels_hbm.1, bf16[4,512]{1,0:T(4,128)(2,1)} %eigs_hbm.1), custom_call_target="tpu_custom_call" | custom-call | tf_op jit(solution)/shard_map/pallas_call | solution.py:427
  55.9 0.8 %copy.6 = bf16[32,10240]{1,0:T(8,128)(2,1)} copy(bf16[32,10240]{1,0:T(8,128)(2,1)S(1)} %shard_map.46) | data formatting | bytes 1310720

commit v8 on v7

--- a/solution.py
+++ b/solution.py
@@ -380,7 +380,10 @@
             def out_block(t):
                 return out.at[:, pl.ds(pl.multiple_of(j * N + c * 256, 256), 256)]
 
-            others(send_out)
+            others_z(send_out)
+            send_out(partner(w, 1, 0))
+            for dz in (4, 3, 5, 2, 6, 1, 7):
+                send_out(partner(w, 1, dz))
             local(own_rows(w), out_block(w), sem_o)
 
     compute(0, w)

time: 56.9 us -> 56.6 us (level); the launches traced: 56.8 us -> 55.5 us
  Pallas kernels: 55.9 us -> 54.7 us
    pallas_call x1, Pallas kernels: 55.9 us -> 54.7 us  [per_device(): pl.pallas_call(kernel, out_shape=jax.ShapeDtypeStruct(grads.shape, BF16),...]
where the time goes in v8:
time: 56.6 us; the launch traced here: 55.5 us
  Pallas kernels  54.7 us (97%)
  local copies, waits for them, and re-layouts  0.84 us (1%)
    pallas_call x1, Pallas kernels, per_device(): pl.pallas_call(kernel, out_shape=jax.ShapeDtypeStruct(grads.shape, BF16),...  54.7 us

profile of v8, /device:TPU:36, one launch (start us, length us, event | category | flops | bytes accessed | tf_op | source)
XLA Modules:
  0.0 55.5 jit_solution(16138964688194294268)
XLA Ops:
  0.0 54.7 %shard_map.46 = bf16[32,10240]{1,0:T(8,128)(2,1)S(1)} custom-call(s32[56]{0:T(128)} %owner_hbm.1, bf16[32,10240]{1,0:T(8,128)(2,1)} %grads_hbm.1, bf16[4,512,512]{2,1,0:T(8,128)(2,1)} %panels_hbm.1, bf16[4,512]{1,0:T(4,128)(2,1)} %eigs_hbm.1), custom_call_target="tpu_custom_call" | custom-call | tf_op jit(solution)/shard_map/pallas_call | solution.py:430
  54.7 0.8 %copy.6 = bf16[32,10240]{1,0:T(8,128)(2,1)} copy(bf16[32,10240]{1,0:T(8,128)(2,1)S(1)} %shard_map.46) | data formatting | bytes 1310720
